TPU v7x, 32 devices: a whole 2x2x4 slice. The times are simulated.
32 devices in a mesh: space: 8 (over y, x, core), ifg: 4 (over z).
Axes of the slice: x: 2, y: 2, z: 4, core: 2. Of those that a mesh axis runs over, the one named last changes fastest.
Arguments:
- phases: float32 [192, 128, 1024], P('ifg', 'space'), may hold values from -12 to 12
- coherence: bfloat16 [192, 128, 1024], P('ifg', 'space'), may hold values from 0.19921875 to 1
- design: int32 [192, 2], replicated, may hold values from 0 to 99, as said below
- geo_lookup: int32 [256, 8], P(('space', 'ifg')), may hold values from -1 to 255, as said below
- geo_weights: bfloat16 [256, 8, 128, 128], P(('space', 'ifg')), may hold values from -0.25 to 0.25
Outputs:
- geo_series: float32 [256, 99, 128], P(('space', 'ifg'))
Inputs may be any that keep to these rules, and one draw needn't show every extreme that they name: `design`: each row names two dates; the second is later than the first by 1 to 3 steps, and some row spans exactly 3. Rows are distinct and every pair of consecutive dates is a row. `geo_lookup`: an entry e >= 0 of a tile owned by device (o, g) names block e % 32 of the pixels that device (e // 32, g) holds after the regrouping; -1 marks an unused entry. Over all tiles of one device, at most 2 entries name blocks of one index of space, a number reached in every draw; in every group g one device's tiles name 2 blocks of every index of space.
All inputs are finite; a program needn't handle non-finite values.
Results may differ from a plain program's by a relative error of at most 0.0029.
Values may be sent and summed in bfloat16 or wider, within the bound.
A program may use at most 64 MiB of HBM per device.

v0:
```python
import functools
import jax
import jax.numpy as jnp
from jax import lax
from jax.experimental import pallas as pl
from jax.experimental.pallas import tpu as pltpu
from jax.sharding import PartitionSpec as P

DATES = 100
SPAN = 3
PASSES = 3
BLOCK = 128
CAP = 2
STEP_SIZE = 0.2
SMOOTHING = 0.3
RIDGE_TERM = 0.2
SEND = jnp.float16


def diffuse_kernel(groups, lanes, u_ref, un_ref, us_ref, c_ref, cn_ref, cs_ref, d_out):
    band = lax.axis_index("space")
    last = lax.axis_size("space") - 1
    chunk, rows, cols = u_ref.shape
    total = rows + 8
    row = lax.broadcasted_iota(jnp.int32, (total, cols), 0)
    col = lax.broadcasted_iota(jnp.int32, (total, cols), 1)
    cut = ((row == total - 1) & (band == 0)) | ((row == rows - 1) & (band == last))
    vert = jnp.where(cut, 0.0, 0.5 * STEP_SIZE)
    east = jnp.where(col == cols - 1, 0.0, 0.5 * STEP_SIZE)
    gap = jnp.zeros((2, cols), jnp.float32)
    grows = rows // groups
    for k in range(chunk):
        u = jnp.concatenate([u_ref[k], us_ref[k], gap, un_ref[k]], axis=0)
        c = jnp.concatenate(
            [
                c_ref[k].astype(jnp.float32),
                cs_ref[k].astype(jnp.float32),
                gap,
                cn_ref[k].astype(jnp.float32),
            ],
            axis=0,
        )
        cv = vert * (c + pltpu.roll(c, total - 1, 0))
        ce = east * (c + pltpu.roll(c, cols - 1, 1))
        for _ in range(PASSES):
            dv = pltpu.roll(u, total - 1, 0) - u
            de = pltpu.roll(u, cols - 1, 1) - u
            fv = cv * dv / (1.0 + 0.25 * (dv * dv))
            fe = ce * de / (1.0 + 0.25 * (de * de))
            u = u + ((fv - pltpu.roll(fv, 1, 0)) + (fe - pltpu.roll(fe, 1, 1)))
        for g in range(groups):
            piece = u[g * grows : (g + 1) * grows]
            piece = jnp.concatenate(
                [piece[:, q * lanes : (q + 1) * lanes] for q in range(cols // lanes)], axis=0
            )
            d_out[g, k] = piece


def regroup_kernel(groups, lanes, c_ref, out):
    chunk, rows, cols = c_ref.shape
    grows = rows // groups
    for k in range(chunk):
        c = c_ref[k].astype(jnp.float32)
        for g in range(groups):
            piece = c[g * grows : (g + 1) * grows]
            piece = jnp.concatenate(
                [piece[:, q * lanes : (q + 1) * lanes] for q in range(cols // lanes)], axis=0
            )
            out[g, k] = piece.astype(out.dtype)


def solve_kernel(nslots, lanes, design, picks, w_ref, d_ref, out, table, low, total):
    ifgs, subs, _ = w_ref.shape
    unknowns = DATES - 1

    def clear(i, _):
        table[i] = -1
        return 0

    lax.fori_loop(0, SPAN * DATES, clear, 0)

    def fill(k, _):
        first = design[k, 0]
        table[(design[k, 1] - first - 1) * DATES + first] = k
        return 0

    lax.fori_loop(0, ifgs, fill, 0)

    def load(t):
        ws, wds = [], []
        for s in range(SPAN):
            k = table[s * DATES + t]
            used = k >= 0
            k = jnp.maximum(k, 0)
            w = jnp.where(used, w_ref[k].astype(jnp.float32), 0.0)
            ws.append(w)
            wds.append(w * d_ref[k].astype(jnp.float32))
        return ws, wds

    ws, wds = load(0)
    zero = ws[0] * 0.0

    def step(j, carry):
        d1, d2, d3, e1, e2, f1, b1, b2, b3 = carry
        (w1, w2, w3), (r1, r2, r3) = load(j + 1)
        diag = jnp.where(
            j == unknowns - 1, 1.0, jnp.where((j == 0) | (j == unknowns - 2), 5.0, 6.0)
        )
        first_off = jnp.where(j == unknowns - 2, -2.0, -4.0)
        a0 = d1 + (w1 + w2 + w3) + (SMOOTHING * diag + RIDGE_TERM)
        a1 = e1 - w1 + jnp.where(j == unknowns - 1, 0.0, SMOOTHING * first_off)
        a2 = f1 - w2 + jnp.where(j >= unknowns - 2, 0.0, SMOOTHING)
        a3 = -w3
        b = b1 - (r1 + r2 + r3)
        inv = 1.0 / a0
        l1, l2, l3 = a1 * inv, a2 * inv, a3 * inv
        low[j, 0], low[j, 1], low[j, 2] = l1, l2, l3
        low[j, 3] = b * inv
        return (
            (d2 + w1) - l1 * a1,
            (d3 + w2) - l2 * a2,
            w3 - l3 * a3,
            e2 - l1 * a2,
            -(l2 * a3),
            -(l1 * a3),
            (b2 + r1) - l1 * b,
            (b3 + r2) - l2 * b,
            r3 - l3 * b,
        )

    lax.fori_loop(0, unknowns, step, (*ws, zero, zero, zero, *wds))

    def back(i, carry):
        x1, x2, x3 = carry
        j = unknowns - 1 - i
        x = low[j, 3] - low[j, 2] * x3 - low[j, 1] * x2 - low[j, 0] * x1
        for q in range(lanes // BLOCK):
            total[q, pl.ds(pl.multiple_of(j * subs, 8), subs), :] = x[
                :, q * BLOCK : (q + 1) * BLOCK
            ]
        return x, x1, x2

    lax.fori_loop(0, unknowns, back, (zero, zero, zero))

    for s in range(nslots):
        row = picks[s, 0]
        tile = picks[s, 1]
        out[s] = total[tile, pl.ds(row, unknowns, stride=subs), :].astype(out.dtype)


def geo_kernel(width, slots, blocks, weights, out):
    t = pl.program_id(0)
    acc = jnp.zeros(out.shape[1:], jnp.float32)
    for j in range(width):
        slot = slots[t * width + j]
        block = blocks[jnp.maximum(slot, 0)]
        block = jnp.where(slot >= 0, block, jnp.zeros_like(block))
        acc = acc + jnp.dot(block, weights[0, j], preferred_element_type=jnp.float32)
    out[0] = acc


def per_device(phases, coherence, design, geo_lookup, geo_weights):
    bands = lax.axis_size("space")
    groups = lax.axis_size("ifg")
    ifgs, rows, cols = phases.shape
    band = lax.axis_index("space")
    unknowns = DATES - 1
    pixels = rows * cols // groups
    nbl = pixels // BLOCK
    lanes = min(256, pixels // 8)
    subs = pixels // lanes
    grows = rows // groups
    tiles, width = geo_lookup.shape

    own = geo_lookup.reshape(1, -1)
    lists = lax.all_gather(own, "space", axis=0, tiled=True)
    entries = lists.shape[1]
    order = jnp.arange(entries, dtype=jnp.int32)
    earlier = order[None, :] < order[:, None]
    mine = (lists >= band * nbl) & (lists < (band + 1) * nbl)
    rank = jnp.sum((mine[:, None, :] & earlier[None]).astype(jnp.int32), axis=2)
    chosen = mine[:, None, :] & (rank[:, None, :] == jnp.arange(CAP, dtype=jnp.int32)[None, :, None])
    picked = jnp.sum(jnp.where(chosen, (lists % nbl)[:, None, :], 0), axis=2).reshape(-1)
    tiles_row = cols // BLOCK
    tiles_lane = lanes // BLOCK
    place = picked % tiles_row
    picks = jnp.stack(
        [picked // tiles_row + grows * (place // tiles_lane), place % tiles_lane], axis=1
    )
    source = jnp.where(own[0] >= 0, own[0] // nbl, -1)
    same = (source[None, :] == source[:, None]) & earlier
    slots = jnp.where(
        own[0] >= 0, source * CAP + jnp.sum(same.astype(jnp.int32), axis=1), -1
    )

    down = [(i, i + 1) for i in range(bands - 1)]
    up = [(i + 1, i) for i in range(bands - 1)]
    cn = lax.ppermute(coherence[:, rows - PASSES :], "space", down)
    cs = lax.ppermute(coherence[:, :PASSES], "space", up)
    un = lax.ppermute(phases[:, rows - PASSES :], "space", down)
    us = lax.ppermute(phases[:, :PASSES], "space", up)

    chunk = 4
    whole = pl.BlockSpec((chunk, rows, cols), lambda i: (i, 0, 0))
    edge = pl.BlockSpec((chunk, PASSES, cols), lambda i: (i, 0, 0))
    regrouped = pl.BlockSpec((groups, chunk, subs, lanes), lambda i: (0, i, 0, 0))
    weights_g = pl.pallas_call(
        functools.partial(regroup_kernel, groups, lanes),
        grid=(ifgs // chunk,),
        in_specs=[whole],
        out_specs=regrouped,
        out_shape=jax.ShapeDtypeStruct((groups, ifgs, subs, lanes), jnp.bfloat16),
        name="regroup",
    )(coherence)
    diffused = pl.pallas_call(
        functools.partial(diffuse_kernel, groups, lanes),
        grid=(ifgs // chunk,),
        in_specs=[whole, edge, edge, whole, edge, edge],
        out_specs=regrouped,
        out_shape=jax.ShapeDtypeStruct((groups, ifgs, subs, lanes), jnp.float32),
        cost_estimate=pl.CostEstimate(
            flops=100 * ifgs * rows * cols, bytes_accessed=10**7, transcendentals=0
        ),
        name="diffuse",
    )(phases, un, us, coherence, cn, cs)
    w = lax.all_to_all(weights_g, "ifg", 0, 0, tiled=True).reshape(-1, subs, lanes)
    d = lax.all_to_all(diffused.astype(SEND), "ifg", 0, 0, tiled=True).reshape(-1, subs, lanes)
    d = d.astype(jnp.float32)

    nslots = bands * CAP
    vmem = pl.BlockSpec(memory_space=pltpu.VMEM)
    smem = pl.BlockSpec(memory_space=pltpu.SMEM)
    send = pl.pallas_call(
        functools.partial(solve_kernel, nslots, lanes),
        in_specs=[smem, smem, vmem, vmem],
        out_specs=vmem,
        out_shape=jax.ShapeDtypeStruct((nslots, unknowns, BLOCK), jnp.bfloat16),
        scratch_shapes=[
            pltpu.SMEM((SPAN * DATES,), jnp.int32),
            pltpu.VMEM((unknowns, 4, subs, lanes), jnp.float32),
            pltpu.VMEM((lanes // BLOCK, unknowns * subs, BLOCK), jnp.float32),
        ],
        compiler_params=pltpu.CompilerParams(vmem_limit_bytes=32 * 2**20),
        name="solve",
    )(design, picks, w, d)
    got = lax.all_to_all(send, "space", 0, 0, tiled=True)

    return pl.pallas_call(
        functools.partial(geo_kernel, width),
        grid_spec=pltpu.PrefetchScalarGridSpec(
            num_scalar_prefetch=1,
            grid=(tiles,),
            in_specs=[
                pl.BlockSpec((nslots, unknowns, BLOCK), lambda t, s: (0, 0, 0)),
                pl.BlockSpec((1, width, BLOCK, geo_weights.shape[3]), lambda t, s: (t, 0, 0, 0)),
            ],
            out_specs=pl.BlockSpec((1, unknowns, geo_weights.shape[3]), lambda t, s: (t, 0, 0)),
        ),
        out_shape=jax.ShapeDtypeStruct((tiles, unknowns, geo_weights.shape[3]), jnp.float32),
        name="geo",
    )(slots, got, geo_weights)


def solution(mesh):
    placed = (
        P("ifg", "space", None),
        P("ifg", "space", None),
        P(),
        P(("space", "ifg"), None),
        P(("space", "ifg"), None, None, None),
    )
    return jax.shard_map(
        per_device,
        mesh=mesh,
        in_specs=placed,
        out_specs=P(("space", "ifg"), None, None),
        check_vma=False,
    )
```

profile of v0, /device:TPU:0, one launch (start us, length us, event | category | flops | bytes accessed | tf_op | source)
XLA Modules:
  0.0 170.6 jit_solution(460120870424099773)
XLA Ops:
  0.0 2.3 %fusion.2 = (f32[48,3,1024]{2,1,0:T(4,128)S(1)}, f32[48,3,1024]{2,1,0:T(4,128)S(1)}) fusion(f32[48,16,1024]{2,1,0:T(8,128)} %u_ref.1), kind=kLoop, calls=%fused_computation.30 | loop fusion | bytes 2359296 | tf_op jit(solution)/shard_map/slice | solution.py:201
  2.6 2.5 %collective-permute-start = (f32[48,3,1024]{2,0,1:T(8,128)S(1)}, f32[48,3,1024]{2,0,1:T(8,128)S(1)}, u32[]{:S(2)}, u32[]{:S(2)}) collective-permute-start(f32[48,3,1024]{2,0,1:T(8,128)S(1)} %copy.33), channel_id=1, source_target_pairs={{0,4},{4,8},{8,12},{12,16},{16,20},{20,24},{24,28},{1,5},{5,9},{9,... | collective-permute-start | bytes 1769480 | tf_op jit(solution)/shard_map/ppermute | solution.py:200
  5.5 1.3 collective-permute-start.1
  7.2 5.1 %collective-permute-start.2 = (bf16[48,3,1024]{2,1,0:T(4,128)(2,1)S(1)}, bf16[48,3,1024]{2,1,0:T(4,128)(2,1)S(1)}, u32[]{:S(2)}, u32[]{:S(2)}) collective-permute-start(bf16[48,3,1024]{2,1,0:T(4,128)(2,1)S(1)} %get-tuple-element.10), channel_id=1, source_target_pairs={{0,4},{4,8},{8,12},{12,16},{16,20},{20,24},{24,28},{1,5},{5,9},{9,... | collective-permute-start | bytes 884744 | tf_op jit(solution)/shard_map/ppermute | solution.py:198
  12.3 1.3 collective-permute-start.3
  13.6 1.3 copy.28.un_ref
  14.9 1.3 copy.29.us_ref
  16.2 0.9 collective-permute-done.3.cs_ref
  17.1 0.8 copy-done.5
  17.9 17.3 %diffuse.1 = f32[4,48,16,256]{3,2,1,0:T(8,128)} custom-call(f32[48,16,1024]{2,1,0:T(8,128)} %u_ref.1, f32[48,3,1024]{2,1,0:T(4,128)} %copy.28.un_ref, f32[48,3,1024]{2,1,0:T(4,128)} %copy.29.us_ref, bf16[48,16,1024]{2,1,0:T(8,128)(2,1)} %c_ref.3, bf16[48,3,1024]{2,1,0:T(4,128)(2,1)} %copy-done.4, bf16[48,3,1024]{2,1,0:T(4,128)(2,1)} %copy-done.5), custom_call_target="tpu_custom_call" | custom-call | flops 78643200 | bytes 10000000 | tf_op jit(solution)/shard_map/diffuse/pallas_call | solution.py:215
  35.2 3.4 %convert_element_type.16 = f16[4,48,16,256]{3,2,1,0:T(8,128)(2,1)} convert(f32[4,48,16,256]{3,2,1,0:T(8,128)} %diffuse.1) | non-fusion elementwise | flops 786432 | bytes 4718592 | tf_op jit(solution)/shard_map/convert_element_type | solution.py:227
  38.6 4.9 %all-to-all-start.1 = ((f16[4,48,16,256]{3,2,1,0:T(8,128)(2,1)}), f16[4,48,16,256]{3,2,1,0:T(8,128)(2,1)S(1)}, u32[]{:S(2)}, u32[]{:S(2)}) async-start(f16[4,48,16,256]{3,2,1,0:T(8,128)(2,1)} %convert_element_type.16), calls=%async_computation.1 | async-start | bytes 3145728 | tf_op jit(solution)/shard_map/all_to_all | solution.py:227
  43.5 7.5 %regroup.1 = bf16[4,48,16,256]{3,2,1,0:T(8,128)(2,1)} custom-call(bf16[48,16,1024]{2,1,0:T(8,128)(2,1)} %c_ref.3), custom_call_target="tpu_custom_call" | custom-call | tf_op jit(solution)/shard_map/regroup/pallas_call | solution.py:207
  51.0 25.6 %all-to-all-done.1 = f16[4,48,16,256]{3,2,1,0:T(8,128)(2,1)S(1)} async-done(((f16[4,48,16,256]{3,2,1,0:T(8,128)(2,1)}), f16[4,48,16,256]{3,2,1,0:T(8,128)(2,1)S(1)}, u32[]{:S(2)}, u32[]{:S(2)}) %all-to-all-start.1) | async-done | bytes 1572896 | tf_op jit(solution)/shard_map/all_to_all | solution.py:227
  76.6 1.1 copy-done.2
  77.7 4.3 %all-to-all-start = ((bf16[4,48,16,256]{3,2,1,0:T(8,128)(2,1)}), bf16[4,48,16,256]{3,2,1,0:T(8,128)(2,1)}, u32[]{:S(2)}, u32[]{:S(2)}) async-start(bf16[4,48,16,256]{3,2,1,0:T(8,128)(2,1)} %regroup.1), calls=%async_computation | async-start | bytes 3145728 | tf_op jit(solution)/shard_map/all_to_all | solution.py:226
  82.3 25.6 %all-gather = s32[8,1,64]{2,1,0:T(1,128)S(1)} all-gather(s32[1,1,64]{2,1,0:T(1,128)S(1)} %reshape.269), channel_id=1, replica_groups=mesh['space'=8,'ifg'=4] {'space'}, dimensions={0}, use_global_device_ids=true | all-gather | bytes 2304 | tf_op jit(solution)/shard_map/all_gather | solution.py:176
  108.7 1.8 %bitcast_convert_fusion.d_ref = f32[192,16,256]{2,1,0:T(8,128)S(1)} fusion(f16[4,48,16,256]{3,2,1,0:T(8,128)(2,1)} %copy-done.2), kind=kLoop, calls=%fused_computation | loop fusion | flops 786432 | bytes 4718592 | tf_op jit(solution)/shard_map/convert_element_type | solution.py:228
  110.5 8.9 %all-to-all-done = bf16[4,48,16,256]{3,2,1,0:T(8,128)(2,1)} async-done(((bf16[4,48,16,256]{3,2,1,0:T(8,128)(2,1)}), bf16[4,48,16,256]{3,2,1,0:T(8,128)(2,1)}, u32[]{:S(2)}, u32[]{:S(2)}) %all-to-all-start) | async-done | bytes 1572896 | tf_op jit(solution)/shard_map/all_to_all | solution.py:226
  119.4 12.0 %solve.1 = bf16[16,99,128]{2,1,0:T(8,128)(2,1)S(1)} custom-call(s32[192,2]{1,0:T(8,128)S(1)} %copy.30.design, s32[16,2]{1,0:T(8,128)S(1)} %copy.31.picks, bf16[192,16,256]{2,1,0:T(8,128)(2,1)} %bitcast.1.w_ref, f32[192,16,256]{2,1,0:T(8,128)S(1)} %bitcast_convert_fusion.d_ref), custom_call_target="tpu_custom_call" | custom-call | tf_op jit(solution)/shard_map/solve/pallas_call | solution.py:233
  132.3 20.0 %all-to-all-start.2 = ((bf16[16,99,128]{2,1,0:T(8,128)(2,1)}), bf16[16,99,128]{2,1,0:T(8,128)(2,1)S(1)}, u32[]{:S(2)}, u32[]{:S(2)}) async-start(bf16[16,99,128]{2,1,0:T(8,128)(2,1)} %copy-done), calls=%async_computation.2 | async-start | bytes 851968 | tf_op jit(solution)/shard_map/all_to_all | solution.py:246
  153.0 8.0 %all-to-all-done.2.blocks = bf16[16,99,128]{2,1,0:T(8,128)(2,1)S(1)} async-done(((bf16[16,99,128]{2,1,0:T(8,128)(2,1)}), bf16[16,99,128]{2,1,0:T(8,128)(2,1)S(1)}, u32[]{:S(2)}, u32[]{:S(2)}) %all-to-all-start.2) | async-done | bytes 405536 | tf_op jit(solution)/shard_map/all_to_all | solution.py:246
  161.7 7.1 %geo.1 = f32[8,99,128]{2,1,0:T(8,128)} custom-call(s32[64]{0:T(128)} %compare_select_fusion.9.slots, bf16[16,99,128]{2,1,0:T(8,128)(2,1)} %copy-done.3, bf16[8,8,128,128]{3,2,1,0:T(8,128)(2,1)} %weights.1), custom_call_target="tpu_custom_call" | custom-call | tf_op jit(solution)/shard_map/geo/pallas_call | solution.py:248
  168.8 1.8 %copy.32 = f32[8,99,128]{2,0,1:T(8,128)} copy(f32[8,99,128]{2,1,0:T(8,128)} %geo.1) | data formatting | bytes 811008 | tf_op jit(solution)/shard_map/geo/pallas_call | solution.py:248
  (37 shorter events, 4.2 us)
Async XLA Ops:
  2.3 4.6 %copy-start.1 = (bf16[48,16,1024]{2,1,0:T(8,128)(2,1)S(1)}, bf16[48,16,1024]{2,1,0:T(8,128)(2,1)}, u32[]{:S(2)}) copy-start(bf16[48,16,1024]{2,1,0:T(8,128)(2,1)} %c_ref.3) | copy-start | bytes 4718596
  2.6 11.0 %collective-permute-start = (f32[48,3,1024]{2,0,1:T(8,128)S(1)}, f32[48,3,1024]{2,0,1:T(8,128)S(1)}, u32[]{:S(2)}, u32[]{:S(2)}) collective-permute-start(f32[48,3,1024]{2,0,1:T(8,128)S(1)} %copy.33), channel_id=1, source_target_pairs={{0,4},{4,8},{8,12},{12,16},{16,20},{20,24},{24,28},{1,5},{5,9},{9,... | collective-permute-start | bytes 1769480 | tf_op jit(solution)/shard_map/ppermute | solution.py:200
  5.5 9.4 %collective-permute-start.1 = (f32[48,3,1024]{2,0,1:T(8,128)S(1)}, f32[48,3,1024]{2,0,1:T(8,128)S(1)}, u32[]{:S(2)}, u32[]{:S(2)}) collective-permute-start(f32[48,3,1024]{2,0,1:T(8,128)S(1)} %copy.34), channel_id=1, source_target_pairs={{4,0},{8,4},{12,8},{16,12},{20,16},{24,20},{28,24},{5,1},{9,5},{13... | collective-permute-start | bytes 1769480 | tf_op jit(solution)/shard_map/ppermute | solution.py:201
  7.2 9.0 %collective-permute-start.2 = (bf16[48,3,1024]{2,1,0:T(4,128)(2,1)S(1)}, bf16[48,3,1024]{2,1,0:T(4,128)(2,1)S(1)}, u32[]{:S(2)}, u32[]{:S(2)}) collective-permute-start(bf16[48,3,1024]{2,1,0:T(4,128)(2,1)S(1)} %get-tuple-element.10), channel_id=1, source_target_pairs={{0,4},{4,8},{8,12},{12,16},{16,20},{20,24},{24,28},{1,5},{5,9},{9,... | collective-permute-start | bytes 884744 | tf_op jit(solution)/shard_map/ppermute | solution.py:198
  12.3 4.8 %collective-permute-start.3 = (bf16[48,3,1024]{2,1,0:T(4,128)(2,1)S(1)}, bf16[48,3,1024]{2,1,0:T(4,128)(2,1)S(1)}, u32[]{:S(2)}, u32[]{:S(2)}) collective-permute-start(bf16[48,3,1024]{2,1,0:T(4,128)(2,1)S(1)} %get-tuple-element.9), channel_id=1, source_target_pairs={{4,0},{8,4},{12,8},{16,12},{20,16},{24,20},{28,24},{5,1},{9,5},{13... | collective-permute-start | bytes 884744 | tf_op jit(solution)/shard_map/ppermute | solution.py:199
  16.2 0.9 copy-start.4
  17.1 0.8 copy-start.5
  38.6 38.0 %all-to-all-start.1 = ((f16[4,48,16,256]{3,2,1,0:T(8,128)(2,1)}), f16[4,48,16,256]{3,2,1,0:T(8,128)(2,1)S(1)}, u32[]{:S(2)}, u32[]{:S(2)}) async-start(f16[4,48,16,256]{3,2,1,0:T(8,128)(2,1)} %convert_element_type.16), calls=%async_computation.1 | async-start | bytes 3145728 | tf_op jit(solution)/shard_map/all_to_all | solution.py:227
  51.0 31.1 %copy-start.6 = (s32[8,8]{1,0:T(8,128)S(1)}, s32[8,8]{1,0:T(8,128)}, u32[]{:S(2)}) copy-start(s32[8,8]{1,0:T(8,128)} %param.8) | copy-start | bytes 772
  51.0 57.6 %copy-start.7 = (s32[192,2]{0,1:T(2,128)S(1)}, s32[192,2]{0,1:T(2,128)}, u32[]{:S(2)}) copy-start(s32[192,2]{0,1:T(2,128)} %param.7) | copy-start | bytes 4612
  76.6 1.1 copy-start.2
  77.7 41.7 %all-to-all-start = ((bf16[4,48,16,256]{3,2,1,0:T(8,128)(2,1)}), bf16[4,48,16,256]{3,2,1,0:T(8,128)(2,1)}, u32[]{:S(2)}, u32[]{:S(2)}) async-start(bf16[4,48,16,256]{3,2,1,0:T(8,128)(2,1)} %regroup.1), calls=%async_computation | async-start | bytes 3145728 | tf_op jit(solution)/shard_map/all_to_all | solution.py:226
  131.5 0.8 copy-start
  132.3 28.7 %all-to-all-start.2 = ((bf16[16,99,128]{2,1,0:T(8,128)(2,1)}), bf16[16,99,128]{2,1,0:T(8,128)(2,1)S(1)}, u32[]{:S(2)}, u32[]{:S(2)}) async-start(bf16[16,99,128]{2,1,0:T(8,128)(2,1)} %copy-done), calls=%async_computation.2 | async-start | bytes 851968 | tf_op jit(solution)/shard_map/all_to_all | solution.py:246
  161.0 0.8 copy-start.3
where the time goes:
time: 171 us
  Pallas kernels  43.9 us (26%)
  waiting for transfers between devices  43.4 us (25%)
  starting transfers between devices  39.5 us (23%)
  blocking collectives  25.6 us (15%)
  local copies, waits for them, and re-layouts  11.7 us (7%)
  other arithmetic  6.37 us (4%)
    all_to_all x1, waiting for transfers between devices, per_device(): lax.all_to_all(diffused.astype(SEND), 'ifg', 0, 0, tiled=True)  25.6 us
    all_gather x1, blocking collectives, per_device(): lists = lax.all_gather(own, 'space', axis=0, tiled=True)  25.6 us
    all_to_all x1, starting transfers between devices, per_device(): got = lax.all_to_all(send, 'space', 0, 0, tiled=True)  20 us
    pallas_call x1, Pallas kernels, per_device(): pl.pallas_call(functools.partial(diffuse_kernel, groups, lanes), grid=(if...  17.3 us
    pallas_call x1, Pallas kernels, per_device(): pl.pallas_call(functools.partial(solve_kernel, nslots, lanes), in_specs=[...  12 us
    all_to_all x1, waiting for transfers between devices, per_device(): lax.all_to_all(weights_g, 'ifg', 0, 0, tiled=True).reshape(-1, subs, lanes)  8.9 us
    all_to_all x1, waiting for transfers between devices, per_device(): got = lax.all_to_all(send, 'space', 0, 0, tiled=True)  7.97 us
    pallas_call x1, Pallas kernels, per_device(): pl.pallas_call(functools.partial(regroup_kernel, groups, lanes), grid=(if...  7.49 us
  transfers between devices with their start and end apart: 7, of which 4 were waited for; matrix products, arithmetic and copies ran while one was open for 4% of the time, Pallas kernels for 4%

commit v1 on v0

v1 whole, which is shorter than its diff:
```python
import functools
import jax
import jax.numpy as jnp
from jax import lax
from jax.experimental import pallas as pl
from jax.experimental.pallas import tpu as pltpu
from jax.sharding import PartitionSpec as P

DATES = 100
SPAN = 3
PASSES = 3
BLOCK = 128
CAP = 2
STEP_SIZE = 0.2
SMOOTHING = 0.3
RIDGE_TERM = 0.2
OCTAVE = 1280.0
FLOOR = 21.9
UNROLL = 4
MESH = pl.DeviceIdType.MESH


def encode(u):
    size = (jnp.log2(jnp.maximum(jnp.abs(u), 1e-30)) + FLOOR) * OCTAVE + 0.5
    code = jnp.clip(size, 0.0, 32767.0).astype(jnp.int32)
    return jnp.where(u < 0, -code, code).astype(jnp.int16)


def decode(code):
    code = code.astype(jnp.int32).astype(jnp.float32)
    size = jnp.exp2(jnp.abs(code) * (1.0 / OCTAVE) - FLOOR)
    return jnp.where(code > 0, size, jnp.where(code < 0, -size, 0.0))


def lists_kernel(own_ref, out, send_sem, recv_sem, own_sem):
    groups = lax.axis_size("ifg")
    count = lax.axis_size("space") * groups
    me = lax.axis_index("space") * groups + lax.axis_index("ifg")
    barrier = pltpu.get_barrier_semaphore()

    def greet(r, _):
        peer = lax.rem(me + r, count)
        pl.semaphore_signal(
            barrier, inc=1, device_id=(peer // groups, lax.rem(peer, groups)), device_id_type=MESH
        )
        return 0

    lax.fori_loop(1, count, greet, 0)
    pl.semaphore_wait(barrier, count - 1)

    def send(r, _):
        peer = lax.rem(me + r, count)
        pltpu.make_async_remote_copy(
            src_ref=own_ref.at[0],
            dst_ref=out.at[me],
            send_sem=send_sem,
            recv_sem=recv_sem,
            device_id=(peer // groups, lax.rem(peer, groups)),
            device_id_type=MESH,
        ).start()
        return 0

    lax.fori_loop(1, count, send, 0)
    mine = pltpu.make_async_copy(own_ref.at[0], out.at[me], own_sem)
    mine.start()
    mine.wait()
    rest = out.at[pl.ds(0, count - 1)]
    landed = pltpu.make_async_remote_copy(
        src_ref=rest,
        dst_ref=rest,
        send_sem=send_sem,
        recv_sem=recv_sem,
        device_id=(lax.rem(me + 1, count) // groups, lax.rem(me + 1, groups)),
        device_id_type=MESH,
    )
    landed.wait_send()
    landed.wait_recv()


def spread_kernel(
    u_ref, un_ref, us_ref, c_ref, cn_ref, cs_ref, sel_ref, w_out, d_out,
    w_send, d_send, send_w, recv_w, send_d, recv_d, own_sem,
):
    band = lax.axis_index("space")
    last = lax.axis_size("space") - 1
    me = lax.axis_index("ifg")
    groups = lax.axis_size("ifg")
    ifgs, rows, cols = u_ref.shape
    slots = w_out.shape[2]
    barrier = pltpu.get_barrier_semaphore()
    peers = [lax.rem(me + r, groups) for r in range(groups)]
    for r in range(1, groups):
        pl.semaphore_signal(barrier, inc=1, device_id=(band, peers[r]), device_id_type=MESH)
    pl.semaphore_wait(barrier, groups - 1)

    def push(src, dst, span, send_sem, recv_sem, r):
        return pltpu.make_async_remote_copy(
            src_ref=src.at[peers[r], span],
            dst_ref=dst.at[me, span],
            send_sem=send_sem.at[r],
            recv_sem=recv_sem.at[r],
            device_id=(band, peers[r]),
            device_id_type=MESH,
        )

    def tiles(x):
        return jnp.concatenate(
            [x[:, q * BLOCK : (q + 1) * BLOCK] for q in range(cols // BLOCK)], axis=0
        )

    def pick(x):
        return jnp.dot(sel_ref[...], x, preferred_element_type=jnp.float32)

    def weigh(i, _):
        for kk in range(UNROLL):
            k = i * UNROLL + kk
            got = pick(tiles(c_ref[k]))
            for g in range(groups):
                w_send[g, k] = got[g * slots : (g + 1) * slots].astype(w_send.dtype)
        return 0

    lax.fori_loop(0, ifgs // UNROLL, weigh, 0)
    everything = pl.ds(0, ifgs)
    for r in range(1, groups):
        push(w_send, w_out, everything, send_w, recv_w, r).start()
    own_w = pltpu.make_async_copy(w_send.at[me], w_out.at[me], own_sem.at[0])
    own_w.start()

    total = rows + 8
    row = lax.broadcasted_iota(jnp.int32, (total, cols), 0)
    col = lax.broadcasted_iota(jnp.int32, (total, cols), 1)
    cut = ((row == total - 1) & (band == 0)) | ((row == rows - 1) & (band == last))
    vert = jnp.where(cut, 0.0, 0.5 * STEP_SIZE)
    east = jnp.where(col == cols - 1, 0.0, 0.5 * STEP_SIZE)
    gap = jnp.zeros((2, cols), jnp.float32)

    def diffuse(i, _):
        for kk in range(UNROLL):
            k = i * UNROLL + kk
            u = jnp.concatenate([u_ref[k], us_ref[k], gap, un_ref[k]], axis=0)
            c = jnp.concatenate(
                [
                    c_ref[k].astype(jnp.float32),
                    cs_ref[k].astype(jnp.float32),
                    gap,
                    cn_ref[k].astype(jnp.float32),
                ],
                axis=0,
            )
            cv = vert * (c + pltpu.roll(c, total - 1, 0))
            ce = east * (c + pltpu.roll(c, cols - 1, 1))
            for _ in range(PASSES):
                dv = pltpu.roll(u, total - 1, 0) - u
                de = pltpu.roll(u, cols - 1, 1) - u
                fv = cv * dv / (1.0 + 0.25 * (dv * dv))
                fe = ce * de / (1.0 + 0.25 * (de * de))
                u = u + ((fv - pltpu.roll(fv, 1, 0)) + (fe - pltpu.roll(fe, 1, 1)))
            u = tiles(u[:rows])
            high = u.astype(jnp.bfloat16)
            got = pick(high) + pick((u - high.astype(jnp.float32)).astype(jnp.bfloat16))
            for g in range(groups):
                d_send[g, k] = encode(got[g * slots : (g + 1) * slots])
        for r in range(1, groups):
            push(d_send, d_out, pl.ds(i * UNROLL, UNROLL), send_d, recv_d, r).start()
        return 0

    lax.fori_loop(0, ifgs // UNROLL, diffuse, 0)
    own_d = pltpu.make_async_copy(d_send.at[me], d_out.at[me], own_sem.at[1])
    own_d.start()
    own_w.wait()
    own_d.wait()
    for r in range(1, groups):
        push(w_send, w_out, everything, send_w, recv_w, r).wait()
        push(d_send, d_out, everything, send_d, recv_d, r).wait()


def solve_kernel(design, w_ref, d_ref, out, table, low, total):
    ifgs, subs, lanes = w_ref.shape
    unknowns = DATES - 1

    def clear(i, _):
        table[i] = -1
        return 0

    lax.fori_loop(0, SPAN * DATES, clear, 0)

    def fill(k, _):
        first = design[k, 0]
        table[(design[k, 1] - first - 1) * DATES + first] = k
        return 0

    lax.fori_loop(0, ifgs, fill, 0)

    def load(t):
        ws, wds = [], []
        for s in range(SPAN):
            k = table[s * DATES + t]
            used = k >= 0
            k = jnp.maximum(k, 0)
            w = jnp.where(used, w_ref[k].astype(jnp.float32), 0.0)
            ws.append(w)
            wds.append(w * decode(d_ref[k]))
        return ws, wds

    ws, wds = load(0)
    zero = ws[0] * 0.0

    def step(j, carry):
        d1, d2, d3, e1, e2, f1, b1, b2, b3 = carry
        (w1, w2, w3), (r1, r2, r3) = load(j + 1)
        diag = jnp.where(
            j == unknowns - 1, 1.0, jnp.where((j == 0) | (j == unknowns - 2), 5.0, 6.0)
        )
        first_off = jnp.where(j == unknowns - 2, -2.0, -4.0)
        a0 = d1 + (w1 + w2 + w3) + (SMOOTHING * diag + RIDGE_TERM)
        a1 = e1 - w1 + jnp.where(j == unknowns - 1, 0.0, SMOOTHING * first_off)
        a2 = f1 - w2 + jnp.where(j >= unknowns - 2, 0.0, SMOOTHING)
        a3 = -w3
        b = b1 - (r1 + r2 + r3)
        inv = 1.0 / a0
        l1, l2, l3 = a1 * inv, a2 * inv, a3 * inv
        low[j, 0], low[j, 1], low[j, 2] = l1, l2, l3
        low[j, 3] = b * inv
        return (
            (d2 + w1) - l1 * a1,
            (d3 + w2) - l2 * a2,
            w3 - l3 * a3,
            e2 - l1 * a2,
            -(l2 * a3),
            -(l1 * a3),
            (b2 + r1) - l1 * b,
            (b3 + r2) - l2 * b,
            r3 - l3 * b,
        )

    lax.fori_loop(0, unknowns, step, (*ws, zero, zero, zero, *wds))

    def back(i, carry):
        x1, x2, x3 = carry
        j = unknowns - 1 - i
        x = low[j, 3] - low[j, 2] * x3 - low[j, 1] * x2 - low[j, 0] * x1
        total[pl.ds(pl.multiple_of(j * subs, 8), subs), :] = x
        return x, x1, x2

    total[pl.ds(unknowns * subs, (out.shape[1] - unknowns) * subs), :] = jnp.zeros(
        ((out.shape[1] - unknowns) * subs, lanes), jnp.float32
    )
    lax.fori_loop(0, unknowns, back, (zero, zero, zero))
    for s in range(subs):
        out[s] = total[pl.ds(s, out.shape[1], stride=subs), :].astype(out.dtype)


def geo_kernel(width, slots, send, weights, out, blocks, send_sem, recv_sem, own_sem):
    bands = lax.axis_size("space")
    me = lax.axis_index("space")
    group = lax.axis_index("ifg")
    barrier = pltpu.get_barrier_semaphore()
    peers = [lax.rem(me + r, bands) for r in range(bands)]
    for r in range(1, bands):
        pl.semaphore_signal(barrier, inc=1, device_id=(peers[r], group), device_id_type=MESH)
    pl.semaphore_wait(barrier, bands - 1)
    copies = [
        pltpu.make_async_remote_copy(
            src_ref=send.at[pl.ds(peers[r] * CAP, CAP)],
            dst_ref=blocks.at[pl.ds(me * CAP, CAP)],
            send_sem=send_sem.at[r],
            recv_sem=recv_sem.at[r],
            device_id=(peers[r], group),
            device_id_type=MESH,
        )
        for r in range(1, bands)
    ]
    for copy in copies:
        copy.start()
    own = pltpu.make_async_copy(
        send.at[pl.ds(me * CAP, CAP)], blocks.at[pl.ds(me * CAP, CAP)], own_sem
    )
    own.start()
    own.wait()
    for copy in copies:
        copy.wait()
    for t in range(out.shape[0]):
        acc = jnp.zeros((blocks.shape[1], out.shape[2]), jnp.float32)
        for j in range(width):
            slot = slots[t * width + j]
            block = blocks[jnp.maximum(slot, 0)]
            block = jnp.where(slot >= 0, block, jnp.zeros_like(block))
            acc = acc + jnp.dot(block, weights[t, j], preferred_element_type=jnp.float32)
        out[t] = acc[: out.shape[1]]


def per_device(phases, coherence, design, geo_lookup, geo_weights):
    bands = lax.axis_size("space")
    groups = lax.axis_size("ifg")
    ifgs, rows, cols = phases.shape
    band = lax.axis_index("space")
    unknowns = DATES - 1
    padded = (unknowns + 15) // 16 * 16
    pixels = rows * cols // groups
    nbl = pixels // BLOCK
    grows = rows // groups
    tiles, width = geo_lookup.shape
    entries = tiles * width
    nslots = bands * CAP
    vmem = pl.BlockSpec(memory_space=pltpu.VMEM)
    smem = pl.BlockSpec(memory_space=pltpu.SMEM)
    dma = pltpu.SemaphoreType.DMA

    down = [(i, i + 1) for i in range(bands - 1)]
    up = [(i + 1, i) for i in range(bands - 1)]
    cn = lax.ppermute(coherence[:, rows - PASSES :], "space", down)
    cs = lax.ppermute(coherence[:, :PASSES], "space", up)
    un = lax.ppermute(phases[:, rows - PASSES :], "space", down)
    us = lax.ppermute(phases[:, :PASSES], "space", up)

    own = geo_lookup.reshape(-1)
    lists = pl.pallas_call(
        lists_kernel,
        in_specs=[vmem],
        out_specs=vmem,
        out_shape=jax.ShapeDtypeStruct((bands * groups, 8, BLOCK), jnp.int32),
        scratch_shapes=[dma, dma, dma],
        compiler_params=pltpu.CompilerParams(collective_id=0, has_side_effects=True),
        name="lists",
    )(jnp.broadcast_to(jnp.pad(own, (0, BLOCK - entries)), (1, 8, BLOCK)))
    lists = lists[:, 0, :entries].reshape(bands, groups, entries).transpose(1, 0, 2)
    order = jnp.arange(entries, dtype=jnp.int32)
    earlier = order[None, :] < order[:, None]
    mine = (lists >= band * nbl) & (lists < (band + 1) * nbl)
    rank = jnp.sum((mine[:, :, None, :] & earlier).astype(jnp.int32), axis=3)
    chosen = mine[:, :, None] & (
        rank[:, :, None] == jnp.arange(CAP, dtype=jnp.int32)[None, None, :, None]
    )
    picked = jnp.max(jnp.where(chosen, (lists % nbl)[:, :, None], -1), axis=3)
    tiles_row = cols // BLOCK
    group_ids = jnp.arange(groups, dtype=jnp.int32)[:, None, None]
    where = (picked % tiles_row) * rows + grows * group_ids + picked // tiles_row
    where = jnp.where(picked >= 0, where, -1).reshape(-1, 1)
    sel = (where == jnp.arange(rows * tiles_row, dtype=jnp.int32)[None]).astype(jnp.bfloat16)
    source = jnp.where(own >= 0, own // nbl, -1)
    same = (source[None, :] == source[:, None]) & earlier
    slots = jnp.where(own >= 0, source * CAP + jnp.sum(same.astype(jnp.int32), axis=1), -1)

    regrouped = (groups, ifgs, nslots, BLOCK)
    w, d = pl.pallas_call(
        spread_kernel,
        in_specs=[vmem] * 7,
        out_specs=[vmem] * 2,
        out_shape=[
            jax.ShapeDtypeStruct(regrouped, jnp.bfloat16),
            jax.ShapeDtypeStruct(regrouped, jnp.int16),
        ],
        scratch_shapes=[pltpu.VMEM(regrouped, jnp.bfloat16), pltpu.VMEM(regrouped, jnp.int16)]
        + [dma((groups,))] * 4
        + [dma((2,))],
        compiler_params=pltpu.CompilerParams(
            collective_id=1, has_side_effects=True, vmem_limit_bytes=48 * 2**20
        ),
        name="spread",
    )(phases, un, us, coherence, cn, cs, sel)

    send = pl.pallas_call(
        solve_kernel,
        in_specs=[smem, vmem, vmem],
        out_specs=vmem,
        out_shape=jax.ShapeDtypeStruct((nslots, padded, BLOCK), jnp.bfloat16),
        scratch_shapes=[
            pltpu.SMEM((SPAN * DATES,), jnp.int32),
            pltpu.VMEM((unknowns, 4, nslots, BLOCK), jnp.float32),
            pltpu.VMEM((padded * nslots, BLOCK), jnp.float32),
        ],
        compiler_params=pltpu.CompilerParams(vmem_limit_bytes=48 * 2**20),
        name="solve",
    )(design, w.reshape(-1, nslots, BLOCK), d.reshape(-1, nslots, BLOCK))

    return pl.pallas_call(
        functools.partial(geo_kernel, width),
        in_specs=[smem, vmem, vmem],
        out_specs=vmem,
        out_shape=jax.ShapeDtypeStruct((tiles, unknowns, geo_weights.shape[3]), jnp.float32),
        scratch_shapes=[
            pltpu.VMEM((nslots, padded, BLOCK), jnp.bfloat16),
            dma((bands,)),
            dma((bands,)),
            dma,
        ],
        compiler_params=pltpu.CompilerParams(
            collective_id=2, has_side_effects=True, vmem_limit_bytes=32 * 2**20
        ),
        name="geo",
    )(slots, send, geo_weights)


def solution(mesh):
    placed = (
        P("ifg", "space", None),
        P("ifg", "space", None),
        P(),
        P(("space", "ifg"), None),
        P(("space", "ifg"), None, None, None),
    )
    return jax.shard_map(
        per_device,
        mesh=mesh,
        in_specs=placed,
        out_specs=P(("space", "ifg"), None, None),
        check_vma=False,
    )
```

time: 171 us -> 104 us (0.61)
  waiting for transfers between devices: 43.4 us -> 0.02 us
  Pallas kernels: 43.9 us -> 80.7 us
  starting transfers between devices: 39.5 us -> 10.2 us
  blocking collectives: 25.6 us -> 0 us
  other arithmetic: 6.37 us -> 1.17 us
    all_to_all x3 -> x0, waiting for transfers between devices: 42.5 us -> none  [the longest x1 25.6 us: per_device(): lax.all_to_all(diffused.astype(SEND), 'ifg', 0, 0, tiled=True)]
    pallas_call x4, Pallas kernels: 43.9 us -> 80.7 us  [the longest x1 42.4 us: per_device(): pl.pallas_call(spread_kernel, in_specs=[vmem] * 7, out_specs=[vmem] * 2,...]
    all_to_all x3 -> x0, starting transfers between devices: 29.2 us -> none  [the longest x1 20 us: per_device(): got = lax.all_to_all(send, 'space', 0, 0, tiled=True)]
    all_gather x1 -> x0, blocking collectives: 25.6 us -> none  [per_device(): lists = lax.all_gather(own, 'space', axis=0, tiled=True)]
    convert_element_type x2 -> x1, other arithmetic: 5.22 us -> 0.07 us  [per_device(): (where == jnp.arange(rows * tiles_row, dtype=jnp.int32)[None]).astype(jnp...]
    unnamed x20 -> x11, local copies, waits for them, and re-layouts: 4.32 us -> 1.64 us
  transfers between devices with their start and end apart: 7 -> 4, of which waited for: 4 -> 0; matrix products, arithmetic and copies ran while one was open for 4% -> 8% of each run, Pallas kernels for 4% -> 17%
where the time goes in v1:
time: 104 us; the launch traced here: 103 us
  Pallas kernels  80.7 us (78%)
  local copies, waits for them, and re-layouts  10.7 us (10%)
  starting transfers between devices  10.2 us (10%)
  other arithmetic  1.17 us (1%)
    pallas_call x1, Pallas kernels, per_device(): pl.pallas_call(spread_kernel, in_specs=[vmem] * 7, out_specs=[vmem] * 2,...  42.4 us
    pallas_call x1, Pallas kernels, per_device(): pl.pallas_call(lists_kernel, in_specs=[vmem], out_specs=vmem, out_shape=j...  17.3 us
    pallas_call x1, Pallas kernels, per_device(): pl.pallas_call(solve_kernel, in_specs=[smem, vmem, vmem], out_specs=vmem,...  11.1 us
    pallas_call x1, Pallas kernels, per_device(): pl.pallas_call(functools.partial(geo_kernel, width), in_specs=[smem, vmem...  9.92 us
    ppermute x1, starting transfers between devices, per_device(): cn = lax.ppermute(coherence[:, rows - PASSES:], 'space', down)  4.35 us
    ppermute x1, starting transfers between devices, per_device(): un = lax.ppermute(phases[:, rows - PASSES:], 'space', down)  3.31 us
    slice x1, local copies, waits for them, and re-layouts, per_device(): us = lax.ppermute(phases[:, :PASSES], 'space', up)  2.26 us
  transfers between devices with their start and end apart: 4, of which 0 were waited for; matrix products, arithmetic and copies ran while one was open for 8% of the time, Pallas kernels for 17%

profile of v1, /device:TPU:0, one launch (start us, length us, event | category | flops | bytes accessed | tf_op | source)
XLA Modules:
  0.0 103.1 jit_solution(9043592657974160030)
XLA Ops:
  0.0 2.3 %fusion.7 = (f32[48,3,1024]{2,1,0:T(4,128)S(1)}, f32[48,3,1024]{2,1,0:T(4,128)S(1)}) fusion(f32[48,16,1024]{2,1,0:T(8,128)} %u_ref.1), kind=kLoop, calls=%fused_computation.31 | loop fusion | bytes 2359296 | tf_op jit(solution)/shard_map/slice | solution.py:314
  2.3 0.3 copy.43
  2.7 3.3 %collective-permute-start = (f32[48,3,1024]{2,0,1:T(8,128)S(1)}, f32[48,3,1024]{2,0,1:T(8,128)}, u32[]{:S(2)}, u32[]{:S(2)}) collective-permute-start(f32[48,3,1024]{2,0,1:T(8,128)S(1)} %copy.43), channel_id=1, source_target_pairs={{0,4},{4,8},{8,12},{12,16},{16,20},{20,24},{24,28},{1,5},{5,9},{9,... | collective-permute-start | bytes 1769480 | tf_op jit(solution)/shard_map/ppermute | solution.py:313
  6.0 1.1 %copy.44 = f32[48,3,1024]{2,0,1:T(8,128)} copy(f32[48,3,1024]{2,1,0:T(4,128)S(1)} %get-tuple-element.9) | data formatting | bytes 1179648
  7.1 1.3 %collective-permute-start.1 = (f32[48,3,1024]{2,0,1:T(8,128)}, f32[48,3,1024]{2,0,1:T(8,128)}, u32[]{:S(2)}, u32[]{:S(2)}) collective-permute-start(f32[48,3,1024]{2,0,1:T(8,128)} %copy.44), channel_id=1, source_target_pairs={{4,0},{8,4},{12,8},{16,12},{20,16},{24,20},{28,24},{5,1},{9,5},{13... | collective-permute-start | bytes 1769480 | tf_op jit(solution)/shard_map/ppermute | solution.py:314
  8.4 1.1 %fusion.8 = (bf16[48,3,1024]{2,1,0:T(4,128)(2,1)S(1)}, bf16[48,3,1024]{2,1,0:T(4,128)(2,1)}) fusion(bf16[48,16,1024]{2,1,0:T(8,128)(2,1)S(1)} %copy-done), kind=kLoop, calls=%fused_computation.32 | loop fusion | bytes 1179648 | tf_op jit(solution)/shard_map/slice | solution.py:312
  9.5 4.3 %collective-permute-start.2 = (bf16[48,3,1024]{2,1,0:T(4,128)(2,1)}, bf16[48,3,1024]{2,1,0:T(4,128)(2,1)S(1)}, u32[]{:S(2)}, u32[]{:S(2)}) collective-permute-start(bf16[48,3,1024]{2,1,0:T(4,128)(2,1)} %get-tuple-element.12), channel_id=1, source_target_pairs={{0,4},{4,8},{8,12},{12,16},{16,20},{20,24},{24,28},{1,5},{5,9},{9,... | collective-permute-start | bytes 884744 | tf_op jit(solution)/shard_map/ppermute | solution.py:311
  13.8 1.3 %collective-permute-start.3 = (bf16[48,3,1024]{2,1,0:T(4,128)(2,1)S(1)}, bf16[48,3,1024]{2,1,0:T(4,128)(2,1)S(1)}, u32[]{:S(2)}, u32[]{:S(2)}) collective-permute-start(bf16[48,3,1024]{2,1,0:T(4,128)(2,1)S(1)} %get-tuple-element.11), channel_id=1, source_target_pairs={{4,0},{8,4},{12,8},{16,12},{20,16},{24,20},{28,24},{5,1},{9,5},{13... | collective-permute-start | bytes 884744 | tf_op jit(solution)/shard_map/ppermute | solution.py:312
  15.3 0.6 broadcast_in_dim.17.own_ref
  15.9 17.3 %lists.1 = s32[32,8,128]{2,1,0:T(8,128)} custom-call(s32[1,8,128]{2,1,0:T(8,128)} %broadcast_in_dim.17.own_ref), custom_call_target="tpu_custom_call" | custom-call | tf_op jit(solution)/shard_map/lists/pallas_call | solution.py:317
  33.2 0.9 slice.19
  34.1 0.6 convert_reduce_fusion
  34.8 0.2 select_reduce_fusion
  35.0 0.1 copy.38
  35.1 0.1 reduce_max.12
  35.3 0.1 add.64
  35.4 0.2 convert_reduce_fusion.1
  35.6 0.1 copy.41.design
  35.8 1.5 %copy.39.un_ref = f32[48,3,1024]{2,1,0:T(4,128)S(1)} copy(f32[48,3,1024]{2,0,1:T(8,128)} %collective-permute-done) | data formatting | bytes 1179648 | tf_op jit(solution)/shard_map/ppermute | solution.py:313
  37.3 1.5 %copy.40.us_ref = f32[48,3,1024]{2,1,0:T(4,128)S(1)} copy(f32[48,3,1024]{2,0,1:T(8,128)} %collective-permute-done.1) | data formatting | bytes 1179648 | tf_op jit(solution)/shard_map/ppermute | solution.py:314
  38.8 42.4 %spread.1 = (bf16[4,48,16,128]{3,2,1,0:T(8,128)(2,1)S(1)}, s16[4,48,16,128]{3,2,1,0:T(8,128)(2,1)S(1)}) custom-call(f32[48,16,1024]{2,1,0:T(8,128)} %u_ref.1, f32[48,3,1024]{2,1,0:T(4,128)S(1)} %copy.39.un_ref, f32[48,3,1024]{2,1,0:T(4,128)S(1)} %copy.40.us_ref, bf16[48,16,1024]{2,1,0:T(8,128)(2,1)S(1)} %copy-done, ...), custom_call_target="tpu_custom_call" | custom-call | tf_op jit(solution)/shard_map/spread/pallas_call | solution.py:345
  81.2 11.1 %solve.1.send = bf16[16,112,128]{2,1,0:T(8,128)(2,1)S(1)} custom-call(s32[192,2]{1,0:T(8,128)S(1)} %copy.41.design, bf16[192,16,128]{2,1,0:T(8,128)(2,1)S(1)} %bitcast.13, s16[192,16,128]{2,1,0:T(8,128)(2,1)S(1)} %bitcast.14), custom_call_target="tpu_custom_call" | custom-call | tf_op jit(solution)/shard_map/solve/pallas_call | solution.py:362
  92.3 9.9 %geo.1 = f32[8,99,128]{2,1,0:T(8,128)S(1)} custom-call(s32[64]{0:T(128)S(1)} %compare_select_fusion.7.slots, bf16[16,112,128]{2,1,0:T(8,128)(2,1)S(1)} %solve.1.send, bf16[8,8,128,128]{3,2,1,0:T(8,128)(2,1)S(1)} %copy-done.1), custom_call_target="tpu_custom_call" | custom-call | tf_op jit(solution)/shard_map/geo/pallas_call | solution.py:376
  102.3 0.8 copy.42
  (23 shorter events, 0.3 us)
Async XLA Ops:
  2.3 6.1 %copy-start = (bf16[48,16,1024]{2,1,0:T(8,128)(2,1)S(1)}, bf16[48,16,1024]{2,1,0:T(8,128)(2,1)}, u32[]{:S(2)}) copy-start(bf16[48,16,1024]{2,1,0:T(8,128)(2,1)} %c_ref.1) | copy-start | bytes 4718596
  2.3 12.9 %copy-start.2 = (s32[8,8]{1,0:T(8,128)S(1)}, s32[8,8]{1,0:T(8,128)}, u32[]{:S(2)}) copy-start(s32[8,8]{1,0:T(8,128)} %param.8) | copy-start | bytes 772
  2.3 33.3 %copy-start.3 = (s32[192,2]{0,1:T(2,128)S(1)}, s32[192,2]{0,1:T(2,128)}, u32[]{:S(2)}) copy-start(s32[192,2]{0,1:T(2,128)} %param.7) | copy-start | bytes 4612
  2.7 33.2 %collective-permute-start = (f32[48,3,1024]{2,0,1:T(8,128)S(1)}, f32[48,3,1024]{2,0,1:T(8,128)}, u32[]{:S(2)}, u32[]{:S(2)}) collective-permute-start(f32[48,3,1024]{2,0,1:T(8,128)S(1)} %copy.43), channel_id=1, source_target_pairs={{0,4},{4,8},{8,12},{12,16},{16,20},{20,24},{24,28},{1,5},{5,9},{9,... | collective-permute-start | bytes 1769480 | tf_op jit(solution)/shard_map/ppermute | solution.py:313
  7.1 30.2 %collective-permute-start.1 = (f32[48,3,1024]{2,0,1:T(8,128)}, f32[48,3,1024]{2,0,1:T(8,128)}, u32[]{:S(2)}, u32[]{:S(2)}) collective-permute-start(f32[48,3,1024]{2,0,1:T(8,128)} %copy.44), channel_id=1, source_target_pairs={{4,0},{8,4},{12,8},{16,12},{20,16},{24,20},{28,24},{5,1},{9,5},{13... | collective-permute-start | bytes 1769480 | tf_op jit(solution)/shard_map/ppermute | solution.py:314
  9.5 29.3 %collective-permute-start.2 = (bf16[48,3,1024]{2,1,0:T(4,128)(2,1)}, bf16[48,3,1024]{2,1,0:T(4,128)(2,1)S(1)}, u32[]{:S(2)}, u32[]{:S(2)}) collective-permute-start(bf16[48,3,1024]{2,1,0:T(4,128)(2,1)} %get-tuple-element.12), channel_id=1, source_target_pairs={{0,4},{4,8},{8,12},{12,16},{16,20},{20,24},{24,28},{1,5},{5,9},{9,... | collective-permute-start | bytes 884744 | tf_op jit(solution)/shard_map/ppermute | solution.py:311
  13.8 25.0 %collective-permute-start.3 = (bf16[48,3,1024]{2,1,0:T(4,128)(2,1)S(1)}, bf16[48,3,1024]{2,1,0:T(4,128)(2,1)S(1)}, u32[]{:S(2)}, u32[]{:S(2)}) collective-permute-start(bf16[48,3,1024]{2,1,0:T(4,128)(2,1)S(1)} %get-tuple-element.11), channel_id=1, source_target_pairs={{4,0},{8,4},{12,8},{16,12},{20,16},{24,20},{28,24},{5,1},{9,5},{13... | collective-permute-start | bytes 884744 | tf_op jit(solution)/shard_map/ppermute | solution.py:312
  81.2 11.2 %copy-start.1 = (bf16[8,8,128,128]{3,2,1,0:T(8,128)(2,1)S(1)}, bf16[8,8,128,128]{3,2,1,0:T(8,128)(2,1)}, u32[]{:S(2)}) copy-start(bf16[8,8,128,128]{3,2,1,0:T(8,128)(2,1)} %weights.1) | copy-start | bytes 6291460

commit v2 on v1

--- a/solution.py
+++ b/solution.py
@@ -32,54 +32,53 @@
     return jnp.where(code > 0, size, jnp.where(code < 0, -size, 0.0))
 
 
-def lists_kernel(own_ref, out, send_sem, recv_sem, own_sem):
-    groups = lax.axis_size("ifg")
-    count = lax.axis_size("space") * groups
-    me = lax.axis_index("space") * groups + lax.axis_index("ifg")
+def lists_kernel(own_ref, out, send_z, recv_z, send_s, recv_s, own_sem):
+    bands, groups = out.shape[:2]
+    band, me = lax.axis_index("space"), lax.axis_index("ifg")
+    along = [(band, lax.rem(me + r, groups)) for r in range(1, groups)]
+    across = [(lax.rem(band + r, bands), me) for r in range(1, bands)]
     barrier = pltpu.get_barrier_semaphore()
-
-    def greet(r, _):
-        peer = lax.rem(me + r, count)
-        pl.semaphore_signal(
-            barrier, inc=1, device_id=(peer // groups, lax.rem(peer, groups)), device_id_type=MESH
-        )
-        return 0
-
-    lax.fori_loop(1, count, greet, 0)
-    pl.semaphore_wait(barrier, count - 1)
-
-    def send(r, _):
-        peer = lax.rem(me + r, count)
+    for peer in along + across:
+        pl.semaphore_signal(barrier, inc=1, device_id=peer, device_id_type=MESH)
+    pl.semaphore_wait(barrier, groups + bands - 2)
+    first = [
         pltpu.make_async_remote_copy(
-            src_ref=own_ref.at[0],
-            dst_ref=out.at[me],
-            send_sem=send_sem,
-            recv_sem=recv_sem,
-            device_id=(peer // groups, lax.rem(peer, groups)),
+            src_ref=own_ref,
+            dst_ref=out.at[band, pl.ds(me, 1)],
+            send_sem=send_z.at[r],
+            recv_sem=recv_z.at[r],
+            device_id=peer,
             device_id_type=MESH,
-        ).start()
-        return 0
-
-    lax.fori_loop(1, count, send, 0)
-    mine = pltpu.make_async_copy(own_ref.at[0], out.at[me], own_sem)
+        )
+        for r, peer in enumerate(along)
+    ]
+    for copy in first:
+        copy.start()
+    mine = pltpu.make_async_copy(own_ref, out.at[band, pl.ds(me, 1)], own_sem)
     mine.start()
     mine.wait()
-    rest = out.at[pl.ds(0, count - 1)]
-    landed = pltpu.make_async_remote_copy(
-        src_ref=rest,
-        dst_ref=rest,
-        send_sem=send_sem,
-        recv_sem=recv_sem,
-        device_id=(lax.rem(me + 1, count) // groups, lax.rem(me + 1, groups)),
-        device_id_type=MESH,
-    )
-    landed.wait_send()
-    landed.wait_recv()
+    for copy in first:
+        copy.wait()
+    second = [
+        pltpu.make_async_remote_copy(
+            src_ref=out.at[band],
+            dst_ref=out.at[band],
+            send_sem=send_s.at[r],
+            recv_sem=recv_s.at[r],
+            device_id=peer,
+            device_id_type=MESH,
+        )
+        for r, peer in enumerate(across)
+    ]
+    for copy in second:
+        copy.start()
+    for copy in second:
+        copy.wait()
 
 
 def spread_kernel(
-    u_ref, un_ref, us_ref, c_ref, cn_ref, cs_ref, sel_ref, w_out, d_out,
-    w_send, d_send, send_w, recv_w, send_d, recv_d, own_sem,
+    u_ref, c_ref, sel_ref, w_out, d_out, w_send, d_send, up_send, down_send, south, north,
+    send_w, recv_w, send_d, recv_d, send_up, recv_up, send_down, recv_down, own_sem,
 ):
     band = lax.axis_index("space")
     last = lax.axis_size("space") - 1
@@ -91,7 +90,41 @@
     peers = [lax.rem(me + r, groups) for r in range(groups)]
     for r in range(1, groups):
         pl.semaphore_signal(barrier, inc=1, device_id=(band, peers[r]), device_id_type=MESH)
-    pl.semaphore_wait(barrier, groups - 1)
+
+    @pl.when(band > 0)
+    def _():
+        pl.semaphore_signal(barrier, inc=1, device_id=(band - 1, me), device_id_type=MESH)
+
+    @pl.when(band < last)
+    def _():
+        pl.semaphore_signal(barrier, inc=1, device_id=(band + 1, me), device_id_type=MESH)
+
+    beside = (band > 0).astype(jnp.int32) + (band < last).astype(jnp.int32)
+    pl.semaphore_wait(barrier, groups - 1 + beside)
+
+    def shift(i, src, dst, send_sem, recv_sem, to):
+        return pltpu.make_async_remote_copy(
+            src_ref=src.at[i],
+            dst_ref=dst.at[i],
+            send_sem=send_sem.at[i],
+            recv_sem=recv_sem.at[i],
+            device_id=(to, me),
+            device_id_type=MESH,
+        )
+
+    def go_up(i):
+        return shift(i, up_send, south, send_up, recv_up, band - 1)
+
+    def go_down(i):
+        return shift(i, down_send, north, send_down, recv_down, band + 1)
+
+    @pl.when(band == 0)
+    def _():
+        north[...] = jnp.zeros_like(north)
+
+    @pl.when(band == last)
+    def _():
+        south[...] = jnp.zeros_like(south)
 
     def push(src, dst, span, send_sem, recv_sem, r):
         return pltpu.make_async_remote_copy(
@@ -112,17 +145,33 @@
         return jnp.dot(sel_ref[...], x, preferred_element_type=jnp.float32)
 
     def weigh(i, _):
+        tops, ends = [], []
         for kk in range(UNROLL):
             k = i * UNROLL + kk
-            got = pick(tiles(c_ref[k]))
+            c = c_ref[k]
+            got = pick(tiles(c))
             for g in range(groups):
                 w_send[g, k] = got[g * slots : (g + 1) * slots].astype(w_send.dtype)
+            u, c = u_ref[k], c.astype(jnp.float32)
+            tops += [u[:PASSES], c[:PASSES]]
+            ends += [u[rows - PASSES :], c[rows - PASSES :]]
+        for r in range(1, groups):
+            push(w_send, w_out, pl.ds(i * UNROLL, UNROLL), send_w, recv_w, r).start()
+
+        @pl.when(band > 0)
+        def _():
+            up_send[i] = jnp.concatenate(tops, axis=0)
+            go_up(i).start()
+
+        @pl.when(band < last)
+        def _():
+            down_send[i] = jnp.concatenate(ends, axis=0)
+            go_down(i).start()
+
         return 0
 
     lax.fori_loop(0, ifgs // UNROLL, weigh, 0)
     everything = pl.ds(0, ifgs)
-    for r in range(1, groups):
-        push(w_send, w_out, everything, send_w, recv_w, r).start()
     own_w = pltpu.make_async_copy(w_send.at[me], w_out.at[me], own_sem.at[0])
     own_w.start()
 
@@ -135,17 +184,24 @@
     gap = jnp.zeros((2, cols), jnp.float32)
 
     def diffuse(i, _):
+        @pl.when(band > 0)
+        def _():
+            go_up(i).wait_send()
+            go_down(i).wait_recv()
+
+        @pl.when(band < last)
+        def _():
+            go_down(i).wait_send()
+            go_up(i).wait_recv()
+
+        above, below = north[i], south[i]
         for kk in range(UNROLL):
             k = i * UNROLL + kk
-            u = jnp.concatenate([u_ref[k], us_ref[k], gap, un_ref[k]], axis=0)
+            a = 2 * PASSES * kk
+            b, e = a + PASSES, a + 2 * PASSES
+            u = jnp.concatenate([u_ref[k], below[a:b], gap, above[a:b]], axis=0)
             c = jnp.concatenate(
-                [
-                    c_ref[k].astype(jnp.float32),
-                    cs_ref[k].astype(jnp.float32),
-                    gap,
-                    cn_ref[k].astype(jnp.float32),
-                ],
-                axis=0,
+                [c_ref[k].astype(jnp.float32), below[b:e], gap, above[b:e]], axis=0
             )
             cv = vert * (c + pltpu.roll(c, total - 1, 0))
             ce = east * (c + pltpu.roll(c, cols - 1, 1))
@@ -174,22 +230,20 @@
         push(d_send, d_out, everything, send_d, recv_d, r).wait()
 
 
-def solve_kernel(design, w_ref, d_ref, out, table, low, total):
-    ifgs, subs, lanes = w_ref.shape
+def solve_kernel(
+    width, table, slots, w_ref, d_ref, weights, out, low, total, send, blocks,
+    send_sem, recv_sem, own_sem,
+):
+    _, subs, lanes = w_ref.shape
     unknowns = DATES - 1
-
-    def clear(i, _):
-        table[i] = -1
-        return 0
-
-    lax.fori_loop(0, SPAN * DATES, clear, 0)
-
-    def fill(k, _):
-        first = design[k, 0]
-        table[(design[k, 1] - first - 1) * DATES + first] = k
-        return 0
-
-    lax.fori_loop(0, ifgs, fill, 0)
+    padded = send.shape[1]
+    bands = lax.axis_size("space")
+    me = lax.axis_index("space")
+    group = lax.axis_index("ifg")
+    barrier = pltpu.get_barrier_semaphore()
+    peers = [lax.rem(me + r, bands) for r in range(bands)]
+    for r in range(1, bands):
+        pl.semaphore_signal(barrier, inc=1, device_id=(peers[r], group), device_id_type=MESH)
 
     def load(t):
         ws, wds = [], []
@@ -233,7 +287,7 @@
             r3 - l3 * b,
         )
 
-    lax.fori_loop(0, unknowns, step, (*ws, zero, zero, zero, *wds))
+    lax.fori_loop(0, unknowns, step, (*ws, zero, zero, zero, *wds), unroll=3)
 
     def back(i, carry):
         x1, x2, x3 = carry
@@ -242,22 +296,13 @@
         total[pl.ds(pl.multiple_of(j * subs, 8), subs), :] = x
         return x, x1, x2
 
-    total[pl.ds(unknowns * subs, (out.shape[1] - unknowns) * subs), :] = jnp.zeros(
-        ((out.shape[1] - unknowns) * subs, lanes), jnp.float32
-    )
-    lax.fori_loop(0, unknowns, back, (zero, zero, zero))
+    total[pl.ds(unknowns * subs, (padded - unknowns) * subs), :] = jnp.zeros(
+        ((padded - unknowns) * subs, lanes), jnp.float32
+    )
+    lax.fori_loop(0, unknowns, back, (zero, zero, zero), unroll=9)
     for s in range(subs):
-        out[s] = total[pl.ds(s, out.shape[1], stride=subs), :].astype(out.dtype)
-
-
-def geo_kernel(width, slots, send, weights, out, blocks, send_sem, recv_sem, own_sem):
-    bands = lax.axis_size("space")
-    me = lax.axis_index("space")
-    group = lax.axis_index("ifg")
-    barrier = pltpu.get_barrier_semaphore()
-    peers = [lax.rem(me + r, bands) for r in range(bands)]
-    for r in range(1, bands):
-        pl.semaphore_signal(barrier, inc=1, device_id=(peers[r], group), device_id_type=MESH)
+        send[s] = total[pl.ds(s, padded, stride=subs), :].astype(send.dtype)
+
     pl.semaphore_wait(barrier, bands - 1)
     copies = [
         pltpu.make_async_remote_copy(
@@ -306,24 +351,17 @@
     smem = pl.BlockSpec(memory_space=pltpu.SMEM)
     dma = pltpu.SemaphoreType.DMA
 
-    down = [(i, i + 1) for i in range(bands - 1)]
-    up = [(i + 1, i) for i in range(bands - 1)]
-    cn = lax.ppermute(coherence[:, rows - PASSES :], "space", down)
-    cs = lax.ppermute(coherence[:, :PASSES], "space", up)
-    un = lax.ppermute(phases[:, rows - PASSES :], "space", down)
-    us = lax.ppermute(phases[:, :PASSES], "space", up)
-
     own = geo_lookup.reshape(-1)
     lists = pl.pallas_call(
         lists_kernel,
         in_specs=[vmem],
         out_specs=vmem,
-        out_shape=jax.ShapeDtypeStruct((bands * groups, 8, BLOCK), jnp.int32),
-        scratch_shapes=[dma, dma, dma],
+        out_shape=jax.ShapeDtypeStruct((bands, groups, 8, BLOCK), jnp.int32),
+        scratch_shapes=[dma((groups,))] * 2 + [dma((bands,))] * 2 + [dma],
         compiler_params=pltpu.CompilerParams(collective_id=0, has_side_effects=True),
         name="lists",
     )(jnp.broadcast_to(jnp.pad(own, (0, BLOCK - entries)), (1, 8, BLOCK)))
-    lists = lists[:, 0, :entries].reshape(bands, groups, entries).transpose(1, 0, 2)
+    lists = lists[:, :, 0, :entries].transpose(1, 0, 2)
     order = jnp.arange(entries, dtype=jnp.int32)
     earlier = order[None, :] < order[:, None]
     mine = (lists >= band * nbl) & (lists < (band + 1) * nbl)
@@ -344,51 +382,53 @@
     regrouped = (groups, ifgs, nslots, BLOCK)
     w, d = pl.pallas_call(
         spread_kernel,
-        in_specs=[vmem] * 7,
+        in_specs=[vmem] * 3,
         out_specs=[vmem] * 2,
         out_shape=[
             jax.ShapeDtypeStruct(regrouped, jnp.bfloat16),
             jax.ShapeDtypeStruct(regrouped, jnp.int16),
         ],
         scratch_shapes=[pltpu.VMEM(regrouped, jnp.bfloat16), pltpu.VMEM(regrouped, jnp.int16)]
+        + [pltpu.VMEM((ifgs // UNROLL, 2 * PASSES * UNROLL, cols), jnp.float32)] * 4
         + [dma((groups,))] * 4
+        + [dma((ifgs // UNROLL,))] * 4
         + [dma((2,))],
         compiler_params=pltpu.CompilerParams(
             collective_id=1, has_side_effects=True, vmem_limit_bytes=48 * 2**20
         ),
         name="spread",
-    )(phases, un, us, coherence, cn, cs, sel)
-
-    send = pl.pallas_call(
-        solve_kernel,
-        in_specs=[smem, vmem, vmem],
-        out_specs=vmem,
-        out_shape=jax.ShapeDtypeStruct((nslots, padded, BLOCK), jnp.bfloat16),
-        scratch_shapes=[
-            pltpu.SMEM((SPAN * DATES,), jnp.int32),
-            pltpu.VMEM((unknowns, 4, nslots, BLOCK), jnp.float32),
-            pltpu.VMEM((padded * nslots, BLOCK), jnp.float32),
-        ],
-        compiler_params=pltpu.CompilerParams(vmem_limit_bytes=48 * 2**20),
-        name="solve",
-    )(design, w.reshape(-1, nslots, BLOCK), d.reshape(-1, nslots, BLOCK))
+    )(phases, coherence, sel)
+
+    key = (design[:, 1] - design[:, 0] - 1) * DATES + design[:, 0]
+    keys = jnp.arange(SPAN * DATES, dtype=jnp.int32)[:, None]
+    index = jnp.arange(design.shape[0], dtype=jnp.int32)[None]
+    table = jnp.max(jnp.where(key[None] == keys, index, -1), axis=1)
 
     return pl.pallas_call(
-        functools.partial(geo_kernel, width),
-        in_specs=[smem, vmem, vmem],
+        functools.partial(solve_kernel, width),
+        in_specs=[smem, smem, vmem, vmem, vmem],
         out_specs=vmem,
         out_shape=jax.ShapeDtypeStruct((tiles, unknowns, geo_weights.shape[3]), jnp.float32),
         scratch_shapes=[
+            pltpu.VMEM((unknowns, 4, nslots, BLOCK), jnp.float32),
+            pltpu.VMEM((padded * nslots, BLOCK), jnp.float32),
+            pltpu.VMEM((nslots, padded, BLOCK), jnp.bfloat16),
             pltpu.VMEM((nslots, padded, BLOCK), jnp.bfloat16),
             dma((bands,)),
             dma((bands,)),
             dma,
         ],
         compiler_params=pltpu.CompilerParams(
-            collective_id=2, has_side_effects=True, vmem_limit_bytes=32 * 2**20
+            collective_id=2, has_side_effects=True, vmem_limit_bytes=48 * 2**20
         ),
-        name="geo",
-    )(slots, send, geo_weights)
+        name="solve",
+    )(
+        table,
+        slots,
+        w.reshape(-1, nslots, BLOCK),
+        d.reshape(-1, nslots, BLOCK),
+        geo_weights,
+    )
 
 
 def solution(mesh):

time: 104 us -> 71.9 us (0.69)
  Pallas kernels: 80.7 us -> 64.6 us
  starting transfers between devices: 10.2 us -> 0 us
  local copies, waits for them, and re-layouts: 10.7 us -> 5.68 us
    pallas_call x3 -> x2, Pallas kernels: 63.4 us -> 51.3 us  [the longest x1 40.6 us: per_device(): pl.pallas_call(spread_kernel, in_specs=[vmem] * 3, out_specs=[vmem] * 2,...]
    ppermute x4 -> x0, starting transfers between devices: 10.2 us -> none  [the longest x1 4.35 us: per_device(): cn = lax.ppermute(coherence[:, rows - PASSES:], 'space', down)]
    pallas_call x1, Pallas kernels: 17.3 us -> 13.3 us  [per_device(): pl.pallas_call(lists_kernel, in_specs=[vmem], out_specs=vmem, out_shape=j...]
    ppermute x2 -> x0, local copies, waits for them, and re-layouts: 2.94 us -> none  [the longest x1 1.47 us: per_device(): un = lax.ppermute(phases[:, rows - PASSES:], 'space', down)]
    slice x3 -> x2, local copies, waits for them, and re-layouts: 4.24 us -> 1.68 us  [the longest x1 0.91 us: per_device(): lists = lists[:, :, 0, :entries].transpose(1, 0, 2)]
  transfers between devices with their start and end apart: 4 -> 0, of which waited for: 0 -> 0; matrix products, arithmetic and copies ran while one was open for 8% -> 0% of each run, Pallas kernels for 17% -> 0%
where the time goes in v2:
time: 71.9 us; the launch traced here: 71.7 us
  Pallas kernels  64.6 us (90%)
  local copies, waits for them, and re-layouts  5.68 us (8%)
  other arithmetic  1.3 us (2%)
    pallas_call x1, Pallas kernels, per_device(): pl.pallas_call(spread_kernel, in_specs=[vmem] * 3, out_specs=[vmem] * 2,...  40.6 us
    pallas_call x1, Pallas kernels, per_device(): pl.pallas_call(lists_kernel, in_specs=[vmem], out_specs=vmem, out_shape=j...  13.3 us
    pallas_call x1, Pallas kernels, per_device(): pl.pallas_call(functools.partial(solve_kernel, width), in_specs=[smem, sm...  10.7 us

profile of v2, /device:TPU:0, one launch (start us, length us, event | category | flops | bytes accessed | tf_op | source)
XLA Modules:
  0.0 71.7 jit_solution(11631128211269727209)
XLA Ops:
  0.0 0.8 %reshape.173 = s32[64]{0:T(128)S(1)} reshape(s32[8,8]{1,0:T(8,128)} %param.8) | data formatting | bytes 512 | tf_op jit(solution)/shard_map/reshape | solution.py:354
  0.8 0.2 convert_reduce_fusion.1
  1.0 0.8 %fusion.6 = (s32[192,1]{0,1:T(1,128)S(1)}, s32[192,1]{0,1:T(1,128)S(1)}) fusion(s32[192,2]{0,1:T(2,128)} %param.7), kind=kLoop, calls=%fused_computation.32 | loop fusion | bytes 3072 | tf_op jit(solution)/shard_map/slice | solution.py:402
  1.8 0.1 select_reduce_fusion.table
  1.9 0.6 broadcast_in_dim.29.own_ref
  2.5 0.1 add.76
  2.6 0.1 add.77
  2.7 13.3 %lists.1 = s32[8,4,8,128]{3,2,1,0:T(8,128)} custom-call(s32[1,8,128]{2,1,0:T(8,128)} %broadcast_in_dim.29.own_ref), custom_call_target="tpu_custom_call" | custom-call | tf_op jit(solution)/shard_map/lists/pallas_call | solution.py:355
  16.0 0.9 %slice.12 = s32[8,4,1,64]{3,2,1,0:T(1,128)S(1)} slice(s32[8,4,8,128]{3,2,1,0:T(8,128)} %lists.1), slice={[0:8], [0:4], [0:1], [0:64]} | slice | bytes 16384 | tf_op jit(solution)/shard_map/slice | solution.py:364
  16.9 0.6 convert_reduce_fusion
  17.6 0.2 select_reduce_fusion.1
  17.8 0.1 copy.23
  17.9 0.1 reduce_max.22
  18.0 0.1 fusion.1.sel_ref
  18.1 0.0 copy-start.1
  18.1 1.4 %copy-done.1 = bf16[48,16,1024]{2,1,0:T(8,128)(2,1)S(1)} copy-done((bf16[48,16,1024]{2,1,0:T(8,128)(2,1)S(1)}, bf16[48,16,1024]{2,1,0:T(8,128)(2,1)}, u32[]{:S(2)}) %copy-start.1) | copy-done | bytes 1572888
  19.5 0.0 copy-start
  19.5 40.6 %spread.1 = (bf16[4,48,16,128]{3,2,1,0:T(8,128)(2,1)S(1)}, s16[4,48,16,128]{3,2,1,0:T(8,128)(2,1)S(1)}) custom-call(f32[48,16,1024]{2,1,0:T(8,128)} %u_ref.1, bf16[48,16,1024]{2,1,0:T(8,128)(2,1)S(1)} %copy-done.1, bf16[64,128]{1,0:T(8,128)(2,1)S(1)} %fusion.1.sel_ref), custom_call_target="tpu_custom_call" | custom-call | tf_op jit(solution)/shard_map/spread/pallas_call | solution.py:383
  60.1 0.0 copy-done
  60.1 10.7 %solve.1 = f32[8,99,128]{2,1,0:T(8,128)S(1)} custom-call(s32[300]{0:T(512)S(1)} %select_reduce_fusion.table, s32[64]{0:T(128)S(1)} %compare_select_fusion.7.slots, bf16[192,16,128]{2,1,0:T(8,128)(2,1)S(1)} %bitcast.9, s16[192,16,128]{2,1,0:T(8,128)(2,1)S(1)} %bitcast.10, bf16[8,8,128,128]{3,2,1,0:T(8,128)(2,1)S(1)} %copy-done), custom_call_target="tpu_custom_call" | custom-call | tf_op jit(solution)/shard_map/solve/pallas_call | solution.py:407
  70.9 0.8 %copy.24 = f32[8,99,128]{2,0,1:T(8,128)} copy(f32[8,99,128]{2,1,0:T(8,128)S(1)} %solve.1) | data formatting | bytes 811008 | tf_op jit(solution)/shard_map/solve/pallas_call | solution.py:407
  (11 shorter events, 0.1 us)
Async XLA Ops:
  18.1 1.4 %copy-start.1 = (bf16[48,16,1024]{2,1,0:T(8,128)(2,1)S(1)}, bf16[48,16,1024]{2,1,0:T(8,128)(2,1)}, u32[]{:S(2)}) copy-start(bf16[48,16,1024]{2,1,0:T(8,128)(2,1)} %c_ref.1) | copy-start | bytes 4718596
  19.5 40.6 %copy-start = (bf16[8,8,128,128]{3,2,1,0:T(8,128)(2,1)S(1)}, bf16[8,8,128,128]{3,2,1,0:T(8,128)(2,1)}, u32[]{:S(2)}) copy-start(bf16[8,8,128,128]{3,2,1,0:T(8,128)(2,1)} %weights.1) | copy-start | bytes 6291460

commit v3 on v2

--- a/solution.py
+++ b/solution.py
@@ -208,8 +208,13 @@
             for _ in range(PASSES):
                 dv = pltpu.roll(u, total - 1, 0) - u
                 de = pltpu.roll(u, cols - 1, 1) - u
-                fv = cv * dv / (1.0 + 0.25 * (dv * dv))
-                fe = ce * de / (1.0 + 0.25 * (de * de))
+                av = 1.0 + 0.25 * (dv * dv)
+                ae = 1.0 + 0.25 * (de * de)
+                both = av * ae
+                inv = pl.reciprocal(both, approx=True)
+                inv = inv * (2.0 - both * inv)
+                fv = cv * dv * (ae * inv)
+                fe = ce * de * (av * inv)
                 u = u + ((fv - pltpu.roll(fv, 1, 0)) + (fe - pltpu.roll(fe, 1, 1)))
             u = tiles(u[:rows])
             high = u.astype(jnp.bfloat16)

time: 71.9 us -> 71.9 us (level)
  no operation moved by 1% of the time
where the time goes in v3:
time: 71.9 us; the launch traced here: 71.7 us
  Pallas kernels  64.6 us (90%)
  local copies, waits for them, and re-layouts  5.68 us (8%)
  other arithmetic  1.3 us (2%)
    pallas_call x1, Pallas kernels, per_device(): pl.pallas_call(spread_kernel, in_specs=[vmem] * 3, out_specs=[vmem] * 2,...  40.6 us
    pallas_call x1, Pallas kernels, per_device(): pl.pallas_call(lists_kernel, in_specs=[vmem], out_specs=vmem, out_shape=j...  13.3 us
    pallas_call x1, Pallas kernels, per_device(): pl.pallas_call(functools.partial(solve_kernel, width), in_specs=[smem, sm...  10.7 us

profile of v3, /device:TPU:0, one launch (start us, length us, event | category | flops | bytes accessed | tf_op | source)
XLA Modules:
  0.0 71.7 jit_solution(4039856303335689659)
XLA Ops:
  0.0 0.8 %reshape.173 = s32[64]{0:T(128)S(1)} reshape(s32[8,8]{1,0:T(8,128)} %param.8) | data formatting | bytes 512 | tf_op jit(solution)/shard_map/reshape | solution.py:359
  0.8 0.2 convert_reduce_fusion.1
  1.0 0.8 %fusion.6 = (s32[192,1]{0,1:T(1,128)S(1)}, s32[192,1]{0,1:T(1,128)S(1)}) fusion(s32[192,2]{0,1:T(2,128)} %param.7), kind=kLoop, calls=%fused_computation.32 | loop fusion | bytes 3072 | tf_op jit(solution)/shard_map/slice | solution.py:407
  1.8 0.1 select_reduce_fusion.table
  1.9 0.6 broadcast_in_dim.29.own_ref
  2.5 0.1 add.76
  2.6 0.1 add.77
  2.7 13.3 %lists.1 = s32[8,4,8,128]{3,2,1,0:T(8,128)} custom-call(s32[1,8,128]{2,1,0:T(8,128)} %broadcast_in_dim.29.own_ref), custom_call_target="tpu_custom_call" | custom-call | tf_op jit(solution)/shard_map/lists/pallas_call | solution.py:360
  16.0 0.9 %slice.12 = s32[8,4,1,64]{3,2,1,0:T(1,128)S(1)} slice(s32[8,4,8,128]{3,2,1,0:T(8,128)} %lists.1), slice={[0:8], [0:4], [0:1], [0:64]} | slice | bytes 16384 | tf_op jit(solution)/shard_map/slice | solution.py:369
  16.9 0.6 convert_reduce_fusion
  17.6 0.2 select_reduce_fusion.1
  17.8 0.1 copy.23
  17.9 0.1 reduce_max.22
  18.0 0.1 fusion.1.sel_ref
  18.1 0.0 copy-start.1
  18.1 1.4 %copy-done.1 = bf16[48,16,1024]{2,1,0:T(8,128)(2,1)S(1)} copy-done((bf16[48,16,1024]{2,1,0:T(8,128)(2,1)S(1)}, bf16[48,16,1024]{2,1,0:T(8,128)(2,1)}, u32[]{:S(2)}) %copy-start.1) | copy-done | bytes 1572888
  19.5 0.0 copy-start
  19.5 40.6 %spread.1 = (bf16[4,48,16,128]{3,2,1,0:T(8,128)(2,1)S(1)}, s16[4,48,16,128]{3,2,1,0:T(8,128)(2,1)S(1)}) custom-call(f32[48,16,1024]{2,1,0:T(8,128)} %u_ref.1, bf16[48,16,1024]{2,1,0:T(8,128)(2,1)S(1)} %copy-done.1, bf16[64,128]{1,0:T(8,128)(2,1)S(1)} %fusion.1.sel_ref), custom_call_target="tpu_custom_call" | custom-call | tf_op jit(solution)/shard_map/spread/pallas_call | solution.py:388
  60.1 0.0 copy-done
  60.1 10.7 %solve.1 = f32[8,99,128]{2,1,0:T(8,128)S(1)} custom-call(s32[300]{0:T(512)S(1)} %select_reduce_fusion.table, s32[64]{0:T(128)S(1)} %compare_select_fusion.7.slots, bf16[192,16,128]{2,1,0:T(8,128)(2,1)S(1)} %bitcast.9, s16[192,16,128]{2,1,0:T(8,128)(2,1)S(1)} %bitcast.10, bf16[8,8,128,128]{3,2,1,0:T(8,128)(2,1)S(1)} %copy-done), custom_call_target="tpu_custom_call" | custom-call | tf_op jit(solution)/shard_map/solve/pallas_call | solution.py:412
  70.9 0.8 %copy.24 = f32[8,99,128]{2,0,1:T(8,128)} copy(f32[8,99,128]{2,1,0:T(8,128)S(1)} %solve.1) | data formatting | bytes 811008 | tf_op jit(solution)/shard_map/solve/pallas_call | solution.py:412
  (11 shorter events, 0.1 us)
Async XLA Ops:
  18.1 1.4 %copy-start.1 = (bf16[48,16,1024]{2,1,0:T(8,128)(2,1)S(1)}, bf16[48,16,1024]{2,1,0:T(8,128)(2,1)}, u32[]{:S(2)}) copy-start(bf16[48,16,1024]{2,1,0:T(8,128)(2,1)} %c_ref.1) | copy-start | bytes 4718596
  19.5 40.6 %copy-start = (bf16[8,8,128,128]{3,2,1,0:T(8,128)(2,1)S(1)}, bf16[8,8,128,128]{3,2,1,0:T(8,128)(2,1)}, u32[]{:S(2)}) copy-start(bf16[8,8,128,128]{3,2,1,0:T(8,128)(2,1)} %weights.1) | copy-start | bytes 6291460
